TPU v7x, 32 devices: a whole 2x2x4 slice. The times are simulated.
32 devices in a mesh: lat: 4 (over y, x), lon: 8 (over z, core).
Axes of the slice: x: 2, y: 2, z: 4, core: 2. Of those that a mesh axis runs over, the one named last changes fastest.
Arguments:
- atmosphere: float32 [128, 1536, 256], P('lat', 'lon'), may hold values from -6 to 6
- cutoff_table: int32 [128], P('lat'), may hold values from 1 to 768, as said below
Outputs:
- advanced: float32 [128, 1536, 256], P('lat', 'lon')
Inputs may be any that keep to these rules, and one draw needn't show every extreme that they name: `cutoff_table`: rows that lie 16 or more rows from both poles hold 768 and are left unfiltered; a row of a cap holds at most 34, and the cap row farthest from its pole holds exactly 34.
All inputs are finite; a program needn't handle non-finite values.
Results may differ from a plain program's by a relative error of at most 0.00005.
Values sent between devices are 32-bit elements; how exact they have to be, the bound alone decides.
A program may use at most 128 MiB of HBM per device.

v0:
```python
import math

import jax
import jax.numpy as jnp
from jax import lax
from jax.sharding import PartitionSpec as P

CMAX = 34


courant_zonal = 0.5
courant_meridional = 0.5
diffusion_rate = 0.25
coriolis_rate = 1.0
time_step = 0.1


def extended(block, sides, width):
    for axis, dim in sides:
        count = lax.axis_size(axis)
        forward = [(i, i + 1) for i in range(count - 1)]
        forward.append((count - 1, 0))
        backward = [(target, source) for source, target in forward]
        low = lax.ppermute(
            lax.slice_in_dim(block, block.shape[dim] - width, None, axis=dim), axis, forward
        )
        high = lax.ppermute(lax.slice_in_dim(block, 0, width, axis=dim), axis, backward)
        block = jnp.concatenate([low, block, high], axis=dim)
    return block


def from_behind(value, axis, steps):
    count = lax.axis_size(axis)
    pairs = [(source, (source + steps) % count) for source in range(count)]
    return lax.ppermute(value, axis, pairs)


def tendency_parts(grid, rows, total_lat):
    centre = grid[1:-1, 1:-1]
    east_cell = grid[1:-1, 2:]
    west_cell = grid[1:-1, :-2]
    north_cell = grid[:-2, 1:-1]
    south_cell = grid[2:, 1:-1]
    spacing = jnp.pi / total_lat
    row_float = rows.astype(jnp.float32)
    cos_mid = jnp.sin((row_float + 0.5) * spacing)[:, None, None, None]
    sin_mid = jnp.cos((row_float + 0.5) * spacing)[:, None, None, None]
    cos_north = jnp.sin(row_float * spacing)[:, None, None, None]
    cos_south = jnp.sin((row_float + 1.0) * spacing)[:, None, None, None]
    flux_east = 0.5 * (centre[:, :, 0:1] + east_cell[:, :, 0:1]) * (0.5 * (centre + east_cell))
    flux_west = 0.5 * (west_cell[:, :, 0:1] + centre[:, :, 0:1]) * (0.5 * (west_cell + centre))
    flux_north = (
        0.5
        * (north_cell[:, :, 1:2] + centre[:, :, 1:2])
        * cos_north
        * (0.5 * (north_cell + centre))
    )
    flux_south = (
        0.5
        * (centre[:, :, 1:2] + south_cell[:, :, 1:2])
        * cos_south
        * (0.5 * (centre + south_cell))
    )
    spread = (
        courant_zonal * (flux_east - flux_west) + courant_meridional * (flux_north - flux_south)
    ) / cos_mid
    smooth = diffusion_rate * (north_cell + south_cell - 2.0 * centre)
    turning = (
        coriolis_rate
        * sin_mid
        * jnp.concatenate(
            [centre[:, :, 1:2], -centre[:, :, 0:1], jnp.zeros_like(centre[:, :, 2:])], axis=2
        )
    )
    return (spread, smooth + turning)


def filter_circles(circles, cuts):
    count = circles.shape[1]
    modes = jnp.arange(CMAX)
    phase = modes[:, None] * jnp.arange(count)[None, :] % count
    angles = phase.astype(jnp.float32) * (2.0 * math.pi / count)
    cosine = jnp.cos(angles)
    sine = jnp.sin(angles)
    highest = lax.Precision.HIGHEST
    real_part = jnp.einsum("rnc,mn->rmc", circles, cosine, precision=highest)
    imag_part = jnp.einsum("rnc,mn->rmc", circles, sine, precision=highest)
    factor = jnp.where(modes == 0, 1.0, 2.0).astype(jnp.float32) / count
    weights = jnp.where(modes[None, :] < cuts[:, None], factor[None, :], 0.0)
    smoothed = jnp.einsum("rmc,mn->rnc", real_part * weights[:, :, None], cosine, precision=highest)
    smoothed = smoothed + jnp.einsum(
        "rmc,mn->rnc", imag_part * weights[:, :, None], sine, precision=highest
    )
    return jnp.where((cuts >= count // 2)[:, None, None], circles, smoothed)


def local(atmosphere, cutoff_table):
    lat_rows, lon_cols, chans = atmosphere.shape
    levels = chans // 8
    lat_count = lax.axis_size("lat")
    lat_place = lax.axis_index("lat")
    padded = extended(atmosphere, (("lat", 0), ("lon", 1)), 1)
    edges = jnp.stack([atmosphere[0], atmosphere[-1]])
    mirrored = from_behind(edges, "lon", lax.axis_size("lon") // 2)
    flip = jnp.where(jnp.arange(chans) < 2 * levels, -1.0, 1.0).astype(jnp.float32)
    mirrored = mirrored * flip
    north_row = jnp.where(lat_place == 0, mirrored[0], padded[0, 1:-1])
    south_row = jnp.where(lat_place == lat_count - 1, mirrored[1], padded[-1, 1:-1])
    padded = padded.at[0, 1:-1].set(north_row).at[-1, 1:-1].set(south_row)
    grid = padded.reshape(lat_rows + 2, lon_cols + 2, 8, levels)
    rows = lat_place * lat_rows + jnp.arange(lat_rows)
    spread, rest = tendency_parts(grid, rows, lat_rows * lat_count)
    spread = spread.reshape(lat_rows, lon_cols, chans)
    rest = rest.reshape(lat_rows, lon_cols, chans)
    circles = lax.all_to_all(spread, "lon", split_axis=2, concat_axis=1, tiled=True)
    filtered = lax.all_to_all(
        filter_circles(circles, cutoff_table), "lon", split_axis=1, concat_axis=2, tiled=True
    )
    return atmosphere + time_step * (rest - filtered)


def solution(mesh):
    placed = (P("lat", "lon", None), P("lat"))
    return jax.shard_map(
        local, mesh=mesh, in_specs=placed, out_specs=P("lat", "lon", None), check_vma=False
    )
```

profile of v0, /device:TPU:0, one launch (start us, length us, event | category | flops | bytes accessed | tf_op | source)
XLA Modules:
  0.0 632.4 jit_solution(18336469798245038147)
XLA Ops:
  0.0 8.3 %copy.50 = f32[32,192,256]{1,2,0:T(8,128)} copy(f32[32,192,256]{2,1,0:T(8,128)} %param.6) | data formatting | bytes 12582912 | tf_op args[0]
  8.3 1.1 fusion.63
  9.4 3.9 collective-permute-start.1
  13.3 0.0 collective-permute-start
  13.4 2.7 collective-permute-start.4
  16.0 0.1 sine_multiply_fusion
  16.1 0.6 fusion.64
  16.7 3.3 collective-permute-done.1
  20.0 5.5 collective-permute-done
  25.5 3.9 pad_maximum_fusion
  29.4 5.2 fusion.62
  34.6 3.0 copy.54
  37.6 2.2 collective-permute-start.3
  39.8 3.0 copy.53
  42.8 0.3 collective-permute-start.2
  43.1 0.0 collective-permute-done.3
  43.1 2.8 copy.56
  45.9 2.3 collective-permute-done.2
  48.2 2.8 copy.55
  50.9 10.9 %pad_maximum_fusion.1 = f32[34,194,256]{1,2,0:T(8,128)} fusion(f32[34,1,256]{1,2,0:T(8,128)} %copy.56, f32[1,192,256]{1,2,0:T(8,128)S(1)} %collective-permute-done.1, f32[32,192,256]{1,2,0:T(8,128)} %copy.50, f32[1,192,256]{1,2,0:T(8,128)S(1)} %collective-permute-done, f32[34,1,256]{1,2,0:T(8,128)} %copy.55), kind=kLoop, calls=%fused_computation.1 | loop fusion | flops 6754304 | bytes 13508608 | tf_op jit(solution)/shard_map/concatenate | solution.py:28
  61.9 0.0 collective-permute-done.4
  61.9 0.1 broadcast_multiply_fusion.2
  62.0 0.1 slice_select_fusion
  62.1 3.2 scatter.6
  65.2 1.8 scatter.9
  67.1 6.3 fusion.18
  73.4 22.9 %fusion.4 = f32[32,192,8,32]{1,3,2,0:T(8,128)} fusion(f32[34,194,8,32]{1,3,2,0:T(8,128)} %bitcast.51, f32[32]{0:T(128)S(1)} %get-tuple-element.47, f32[32,192,32]{1,2,0:T(8,128)S(1)} %get-tuple-element.30, f32[32,192,32]{1,2,0:T(8,128)S(1)} %get-tuple-element.33, f32[32,192,32]{1,2,0:T(8,128)} %get-tuple-element.34, f32[32,192,32]{1,2,0:T(8,128)S(1)} %get-tuple-element.29), kind=kLoop, calls=%fused_computation.7 | loop fusion | flops 20447232 | bytes 40894592 | tf_op jit(solution)/shard_map/div | solution.py:64
  96.3 11.5 %copy.57 = f32[32,192,256]{1,0,2:T(8,128)} copy(f32[32,192,256]{1,2,0:T(8,128)} %bitcast.60) | data formatting | bytes 12582912 | tf_op jit(solution)/shard_map/reshape | solution.py:113
  107.8 0.0 copy-start.3
  107.8 5.1 all-to-all-start
  112.9 0.0 copy-done.3
  112.9 0.1 fusion.46
  113.0 183.8 %all-to-all-done = f32[32,192,256]{1,0,2:T(8,128)} async-done(((f32[32,192,256]{1,0,2:T(8,128)}), f32[32,192,256]{1,0,2:T(8,128)}, u32[]{:S(2)}, u32[]{:S(2)}) %all-to-all-start) | async-done | bytes 6291488 | tf_op jit(solution)/shard_map/all_to_all | solution.py:115
  296.8 11.5 %copy.59 = f32[32,8,192,32]{2,1,3,0:T(8,128)} copy(f32[32,8,192,32]{2,0,3,1:T(8,128)} %bitcast.10) | data formatting | bytes 12582912 | tf_op jit(solution)/shard_map/all_to_all | solution.py:115
  308.2 9.5 %all_to_all.27 = f32[32,1536,32]{1,2,0:T(8,128)} reshape(f32[32,8,192,32]{2,1,3,0:T(8,128)} %copy.59) | data formatting | bytes 12582912 | tf_op jit(solution)/shard_map/all_to_all | solution.py:115
  317.8 0.0 copy-start
  317.8 9.2 %fusion.31 = f32[34,1024]{0,1:S(1)} fusion(f32[1536,1024]{0,1:T(8,128)} %bitcast.53), kind=kOutput, calls=%fused_computation.47 | convolution fusion | flops 642198528 | bytes 6430720
  327.0 0.0 copy-done
  327.0 5.2 fusion.27
  332.2 0.1 broadcast_multiply_fusion
  332.4 8.4 %fusion.25 = f32[1536,1024]{0,1} fusion(f32[34,1024]{0,1:T(8,128)S(1)} %bitcast.64), kind=kOutput, calls=%fused_computation.44 | convolution fusion | flops 642198528 | bytes 6430720
  340.8 8.7 %fusion.29 = f32[1536,1024]{0,1} fusion(f32[34,1024]{0,1:T(8,128)S(1)} %bitcast.63), kind=kOutput, calls=%fused_computation.46 | convolution fusion | flops 642198528 | bytes 6430720
  349.4 9.6 %bitcast_select_fusion = f32[32,1536,32]{1,2,0:T(8,128)} fusion(f32[32,1536,32]{1,2,0:T(8,128)S(1)} %copy-done, f32[1536,32,32]{0,2,1:T(8,128)} %bitcast.57, f32[1536,32,32]{0,2,1:T(8,128)} %bitcast.58, pred[32]{0:T(512)(128)(4,1)S(1)} %broadcast_compare_fusion), kind=kLoop, calls=%fused_computation.14 | loop fusion | flops 3145728 | bytes 25165856 | tf_op jit(solution)/shard_map/jit(_where)/select_n | solution.py:94
  359.0 20.4 %copy.60 = f32[32,1536,32]{2,0,1:T(8,128)} copy(f32[32,1536,32]{1,2,0:T(8,128)} %bitcast_select_fusion) | data formatting | bytes 12582912 | tf_op jit(solution)/shard_map/jit(_where)/select_n | solution.py:94
  379.4 16.7 %reshape.173 = f32[8,1,196608]{2,1,0:T(1,128)} reshape(f32[1536,32,32]{2,1,0:T(8,128)} %bitcast.55) | data formatting | bytes 12582912
  396.1 5.0 all-to-all-start.1
  401.1 0.1 pad.10.clone
  401.2 138.9 %all-to-all-done.1 = f32[8,1,196608]{2,1,0:T(1,128)} async-done(((f32[8,1,196608]{2,1,0:T(1,128)}), f32[8,1,196608]{2,1,0:T(1,128)}, u32[]{:S(2)}, u32[]{:S(2)}) %all-to-all-start.1) | async-done | bytes 6291488 | tf_op jit(solution)/shard_map/all_to_all | solution.py:116
  540.0 0.6 broadcast.179
  540.6 19.5 %reduce.4 = f32[8,196608]{1,0:T(8,128)} reduce(f32[8,1,196608]{2,1,0:T(1,128)} %all-to-all-done.1, f32[]{:T(128)} %broadcast.179), dimensions={1}, to_apply=%all_to_all.28.reduce_sub_computation | reduce | bytes 12582916 | tf_op jit(solution)/shard_map/all_to_all | solution.py:116
  560.2 19.2 %reshape.174 = f32[1536,32,32]{2,1,0:T(8,128)} reshape(f32[8,196608]{1,0:T(8,128)} %reduce.4) | data formatting | bytes 12582912
  579.4 0.0 copy-start.1
  579.4 0.0 copy-start.2
  579.4 18.5 %copy.62 = f32[32,8,192,32]{2,3,1,0:T(8,128)} copy(f32[32,8,192,32]{3,0,2,1:T(8,128)} %bitcast.56) | data formatting | bytes 12582912 | tf_op jit(solution)/shard_map/all_to_all | solution.py:116
  597.9 0.0 copy-done.1
  597.9 0.0 copy-done.2
  597.9 17.2 %fusion.8 = f32[32,192,8,32]{1,3,2,0:T(8,128)} fusion(f32[32,192,1,32]{1,3,2,0:T(8,128)S(1)} %copy-done.1, f32[32,192,1,32]{1,3,2,0:T(8,128)S(1)} %copy-done.2, f32[32,8,192,32]{2,3,1,0:T(8,128)} %copy.62, f32[34,194,8,32]{1,3,2,0:T(8,128)} %bitcast.52, f32[8]{0:T(128)S(1)} %pad.10.clone, f32[32]{0:T(128)S(1)} %get-tuple-element.48), kind=kLoop, calls=%fused_computation.13 | loop fusion | flops 15728640 | bytes 33030304 | tf_op jit(solution)/shard_map/mul | solution.py:119
  615.1 8.3 %copy.63 = f32[32,192,256]{2,1,0:T(8,128)} copy(f32[32,192,256]{1,2,0:T(8,128)} %bitcast.59) | data formatting | bytes 12582912 | tf_op jit(solution)/shard_map/mul | solution.py:119
  623.5 8.4 %add.118 = f32[32,192,256]{2,1,0:T(8,128)} add(f32[32,192,256]{2,1,0:T(8,128)} %param.6, f32[32,192,256]{2,1,0:T(8,128)} %copy.63) | non-fusion elementwise | flops 1572864 | bytes 18874368 | tf_op jit(solution)/shard_map/add | solution.py:119
  (7 shorter events, 0.1 us)
Async XLA Ops:
  9.4 10.7 %collective-permute-start.1 = (f32[1,192,256]{1,2,0:T(8,128)S(1)}, f32[1,192,256]{1,2,0:T(8,128)S(1)}, u32[]{:S(2)}, u32[]{:S(2)}) collective-permute-start(f32[1,192,256]{1,2,0:T(8,128)S(1)} %get-tuple-element.38), channel_id=1, source_target_pairs={{8,0},{16,8},{24,16},{0,24},{9,1},{17,9},{25,17},{1,25},{10,2},{18... | collective-permute-start | bytes 589832 | tf_op jit(solution)/shard_map/ppermute | solution.py:27
  13.3 12.2 %collective-permute-start = (f32[1,192,256]{1,2,0:T(8,128)S(1)}, f32[1,192,256]{1,2,0:T(8,128)S(1)}, u32[]{:S(2)}, u32[]{:S(2)}) collective-permute-start(f32[1,192,256]{1,2,0:T(8,128)S(1)} %get-tuple-element.37), channel_id=1, source_target_pairs={{0,8},{8,16},{16,24},{24,0},{1,9},{9,17},{17,25},{25,1},{2,10},{10... | collective-permute-start | bytes 589832 | tf_op jit(solution)/shard_map/ppermute | solution.py:24
  13.4 48.5 %collective-permute-start.4 = (f32[2,192,256]{1,2,0:T(8,128)S(1)}, f32[2,192,256]{1,2,0:T(8,128)S(1)}, u32[]{:S(2)}, u32[]{:S(2)}) collective-permute-start(f32[2,192,256]{1,2,0:T(8,128)S(1)} %pad_maximum_fusion.2), channel_id=1, source_target_pairs={{0,4},{1,5},{2,6},{3,7},{4,0},{5,1},{6,2},{7,3},{8,12},{9,13},{10,... | collective-permute-start | bytes 1179656 | tf_op jit(solution)/shard_map/ppermute | solution.py:35
  37.6 5.5 collective-permute-start.3
  42.8 5.4 collective-permute-start.2
  107.8 5.1 copy-start.3
  107.8 189.0 %all-to-all-start = ((f32[32,192,256]{1,0,2:T(8,128)}), f32[32,192,256]{1,0,2:T(8,128)}, u32[]{:S(2)}, u32[]{:S(2)}) async-start(f32[32,192,256]{1,0,2:T(8,128)} %copy.57), calls=%async_computation | async-start | bytes 16777216 | tf_op jit(solution)/shard_map/all_to_all | solution.py:115
  317.8 9.2 %copy-start = (f32[32,1536,32]{1,2,0:T(8,128)S(1)}, f32[32,1536,32]{1,2,0:T(8,128)}, u32[]{:S(2)}) copy-start(f32[32,1536,32]{1,2,0:T(8,128)} %all_to_all.27) | copy-start | bytes 18874372
  396.1 144.0 %all-to-all-start.1 = ((f32[8,1,196608]{2,1,0:T(1,128)}), f32[8,1,196608]{2,1,0:T(1,128)}, u32[]{:S(2)}, u32[]{:S(2)}) async-start(f32[8,1,196608]{2,1,0:T(1,128)} %reshape.173), calls=%async_computation.1 | async-start | bytes 12582912 | tf_op jit(solution)/shard_map/all_to_all | solution.py:116
  579.4 18.5 %copy-start.1 = (f32[32,192,1,32]{1,3,2,0:T(8,128)S(1)}, f32[32,192,1,32]{1,3,2,0:T(8,128)}, u32[]{:S(2)}) copy-start(f32[32,192,1,32]{1,3,2,0:T(8,128)} %get-tuple-element.31) | copy-start | bytes 2359300
  579.4 18.5 %copy-start.2 = (f32[32,192,1,32]{1,3,2,0:T(8,128)S(1)}, f32[32,192,1,32]{1,3,2,0:T(8,128)}, u32[]{:S(2)}) copy-start(f32[32,192,1,32]{1,3,2,0:T(8,128)} %get-tuple-element.32) | copy-start | bytes 2359300
where the time goes:
time: 637 us; the launch traced here: 632 us
  waiting for transfers between devices  334 us (52%)
  local copies, waits for them, and re-layouts  148 us (23%)
  other arithmetic  99.3 us (16%)
  matrix products  31.5 us (5%)
  starting transfers between devices  19.2 us (3%)
    all_to_all x1, waiting for transfers between devices, local(): lax.all_to_all(spread, 'lon', split_axis=2, concat_axis=1, tiled=True)  184 us
    all_to_all x1, waiting for transfers between devices, local(): lax.all_to_all(filter_circles(circles, cutoff_table), 'lon', split_axis=1...  139 us
    unnamed x11, local copies, waits for them, and re-layouts  44.2 us
    unnamed x4, matrix products  31.5 us
    div x1, other arithmetic, tendency_parts(): (courant_zonal * (flux_east - flux_west) + courant_meridional * (flux_nor...  22.9 us
    all_to_all x2, local copies, waits for them, and re-layouts, local(): lax.all_to_all(spread, 'lon', split_axis=2, concat_axis=1, tiled=True)  21 us
    select_n x1, local copies, waits for them, and re-layouts, filter_circles(): return jnp.where((cuts >= count // 2)[:, None, None], circles, smoothed)  20.4 us
    all_to_all x1, other arithmetic, local(): lax.all_to_all(filter_circles(circles, cutoff_table), 'lon', split_axis=1...  19.5 us
  transfers between devices with their start and end apart: 7, of which 5 were waited for; matrix products, arithmetic and copies ran while one was open for 5% of the time, Pallas kernels for 0%

commit v1 on v0

v1 whole, which is shorter than its diff:
```python
import functools
import math

import jax
import jax.numpy as jnp
import ml_dtypes
import numpy as np
from jax import lax
from jax.experimental import pallas as pl
from jax.experimental.pallas import tpu as pltpu
from jax.sharding import PartitionSpec as P

CMAX = 34
POLAR = 16
CHUNKS = POLAR // 2
COEF = 72
PAD = 8
MESH = pl.DeviceIdType.MESH

courant_zonal = 0.5
courant_meridional = 0.5
diffusion_rate = 0.25
coriolis_rate = 1.0
time_step = 0.1


def row_table(total_lat):
    rows = np.arange(total_lat, dtype=np.float64)
    spacing = np.pi / total_lat
    cos_mid = np.sin((rows + 0.5) * spacing)
    zonal = 0.25 * courant_zonal / cos_mid
    north = 0.25 * courant_meridional * np.sin(rows * spacing) / cos_mid
    south = 0.25 * courant_meridional * np.sin((rows + 1.0) * spacing) / cos_mid
    turning = time_step * coriolis_rate * np.cos((rows + 0.5) * spacing)
    return np.concatenate([zonal, north, south, turning]).astype(np.float32)


def split16(values):
    high = values.astype(ml_dtypes.bfloat16)
    low = (values - high.astype(np.float64)).astype(ml_dtypes.bfloat16)
    return high, low


def fourier_tables(lon_count, cols):
    total = lon_count * cols
    modes = np.arange(CMAX)
    phase = modes[:, None] * np.arange(total)[None, :] % total
    angles = phase * (2.0 * math.pi / total)
    rows = np.zeros((COEF, total))
    rows[:CMAX] = np.cos(angles)
    rows[CMAX : 2 * CMAX] = np.sin(angles)
    factor = np.zeros((COEF,))
    factor[:CMAX] = np.where(modes == 0, 1.0, 2.0) / total
    factor[CMAX : 2 * CMAX] = factor[:CMAX]
    per_device = rows.reshape(COEF, lon_count, cols).transpose(1, 0, 2)
    high, low = split16(per_device)
    forward = np.concatenate([high, low], axis=1)
    high, low = split16(time_step * (per_device * factor[None, :, None]).transpose(0, 2, 1))
    padded_cols = -(-cols // 16) * 16
    inverse = np.zeros((lon_count, padded_cols, 256), ml_dtypes.bfloat16)
    inverse[:, :cols, :COEF] = high
    inverse[:, :cols, COEF : 2 * COEF] = low
    inverse[:, :cols, 2 * COEF : 3 * COEF] = high
    return forward, inverse


def kernel(
    lat_count, lon_count, levels,
    atm, cuts, table, fwd_hbm, inv_hbm, out,
    grid, stage, spread, fwd, inv, ew_send, ew_recv,
    part, part_in, acc, from_outer, from_inner, total, other_total,
    load_sem, out_sem, tab_sem, halo_send, halo_recv, side_send, side_recv,
    part_send, part_recv, inner_send, outer_send, outer_recv, inner_recv, tot_send, tot_recv,
):
    rows, cols, chans = atm.shape
    lat, lon = lax.axis_index("lat"), lax.axis_index("lon")
    total_lat = lat_count * rows
    block = math.gcd(cols, 48)
    chips = lon_count // 2
    half = chips // 2
    chip, core = lon // 2, lon % 2
    is_right = chip // half
    depth = (1 - is_right) * chip + is_right * (chips - 1 - chip)
    step = 2 - 4 * is_right
    inner = lon + step
    outer = lon - step
    sibling = lon + 1 - 2 * core
    innermost = depth == half - 1
    last = lat // (lat_count - 1)
    polar = jnp.logical_or(lat == 0, lat == lat_count - 1)
    behind = (lon + lon_count // 2) % lon_count

    def wrap(offset):
        return (lon + lon_count + offset) % lon_count

    barrier = pltpu.get_barrier_semaphore()
    for other in (wrap(1), wrap(-1), wrap(2), wrap(-2), behind):
        pl.semaphore_signal(barrier, inc=1, device_id=(lat, other), device_id_type=MESH)

    @pl.when(lat > 0)
    def _():
        pl.semaphore_signal(barrier, inc=1, device_id=(lat - 1, lon), device_id_type=MESH)

    @pl.when(lat < lat_count - 1)
    def _():
        pl.semaphore_signal(barrier, inc=1, device_id=(lat + 1, lon), device_id_type=MESH)

    load = pltpu.make_async_copy(atm, grid.at[pl.ds(1, rows), pl.ds(PAD, cols)], load_sem)
    load.start()

    @pl.when(polar)
    def _():
        pltpu.make_async_copy(fwd_hbm.at[lon], fwd, tab_sem.at[0]).start()
        pltpu.make_async_copy(inv_hbm.at[lon], inv, tab_sem.at[1]).start()

    ends = (lat == 0).astype(jnp.int32) + (lat == lat_count - 1).astype(jnp.int32)
    pl.semaphore_wait(barrier, 7 - ends)

    def remote(src, dst, send, recv, to_lat, to_lon):
        return pltpu.make_async_remote_copy(
            src_ref=src, dst_ref=dst, send_sem=send, recv_sem=recv,
            device_id=(to_lat, to_lon), device_id_type=MESH,
        )

    def row_copy(source_row, ghost_row, send_slot, recv_slot, to_lat, to_lon):
        return remote(
            atm.at[source_row], grid.at[ghost_row, pl.ds(PAD, cols)],
            halo_send.at[send_slot], halo_recv.at[recv_slot], to_lat, to_lon,
        )

    @pl.when(lat == 0)
    def _():
        row_copy(0, 0, 0, 0, lat, behind).start()

    @pl.when(lat > 0)
    def _():
        row_copy(0, rows + 1, 0, 1, lat - 1, lon).start()

    @pl.when(lat < lat_count - 1)
    def _():
        row_copy(rows - 1, 0, 1, 0, lat + 1, lon).start()

    @pl.when(lat == lat_count - 1)
    def _():
        row_copy(rows - 1, rows + 1, 1, 1, lat, behind).start()

    load.wait()
    ew_send[0] = grid[1 : rows + 1, PAD : PAD + 1, :]
    ew_send[1] = grid[1 : rows + 1, PAD + cols - 1 : PAD + cols, :]
    to_west = remote(ew_send.at[0], ew_recv.at[1], side_send.at[0], side_recv.at[1], lat, wrap(-1))
    to_east = remote(ew_send.at[1], ew_recv.at[0], side_send.at[1], side_recv.at[0], lat, wrap(1))
    to_west.start()
    to_east.start()
    to_west.wait_recv()
    to_east.wait_recv()
    grid[1 : rows + 1, PAD - 1 : PAD, :] = ew_recv[0]
    grid[1 : rows + 1, PAD + cols : PAD + cols + 1, :] = ew_recv[1]

    lane = lax.broadcasted_iota(jnp.int32, (block, 128), 1)
    is_u = lane < levels
    is_v = jnp.logical_and(lane >= levels, lane < 2 * levels)

    def repeated(value, mask):
        value = jnp.where(mask, value, 0.0)
        value = value + pltpu.roll(value, levels, 1)
        return value + pltpu.roll(value, 2 * levels, 1)

    def wait_ghost(side):
        row_copy(0, side * (rows + 1), side, side, lat, lon_count - 1 - lon).wait_recv()

    def flip_ghost(row):
        winds = grid[row, PAD : PAD + cols, 0:128]
        lanes = lax.broadcasted_iota(jnp.int32, (cols, 128), 1)
        grid[row, PAD : PAD + cols, 0:128] = jnp.where(lanes < 2 * levels, -winds, winds)

    def row_step(i, filtered):
        row = lat * rows + i
        zonal = table[row]
        north = table[total_lat + row]
        south = table[2 * total_lat + row]
        turn = table[3 * total_lat + row]
        for first in range(PAD, PAD + cols, block):
            winds = None
            for h in range(chans // 128):
                lanes = slice(h * 128, h * 128 + 128)
                q = grid[i + 1, first : first + block, lanes]
                q_n = grid[i, first : first + block, lanes]
                q_s = grid[i + 2, first : first + block, lanes]
                east = q + grid[i + 1, first + 1 : first + 1 + block, lanes]
                west = q + grid[i + 1, first - 1 : first - 1 + block, lanes]
                above = q + q_n
                below = q + q_s
                base = (1.0 - 4.0 * diffusion_rate * time_step) * q
                base = base + (diffusion_rate * time_step) * (above + below)
                if h == 0:
                    winds = (
                        repeated(zonal * east, is_u), repeated(zonal * west, is_u),
                        repeated(north * above, is_v), repeated(south * below, is_v),
                    )
                    v = pltpu.roll(q, 128 - levels, 1)
                    u = pltpu.roll(q, levels, 1)
                    base = base + turn * jnp.where(is_u, v, jnp.where(is_v, -u, 0.0))
                u_e, u_w, v_n, v_s = winds
                value = (u_e * east - u_w * west) + (v_n * above - v_s * below)
                columns = slice(first - PAD, first - PAD + block)
                if filtered:
                    stage[i, columns, lanes] = base
                    spread[columns, lanes] = value
                else:
                    stage[i, columns, lanes] = base - time_step * value

    def send_row(i):
        pltpu.make_async_copy(stage.at[i], out.at[i], out_sem).start()

    def plain_row(i):
        row_step(i, False)
        send_row(i)

    def coefficients(i):
        row_step(i, True)
        value = spread[...]
        high = value.astype(jnp.bfloat16)
        low = (value - high.astype(jnp.float32)).astype(jnp.bfloat16)
        weights = fwd[...]
        both = jnp.dot(weights, high, preferred_element_type=jnp.float32)
        both = both + jnp.dot(weights, low, preferred_element_type=jnp.float32)
        return both[:COEF] + both[COEF:]

    def finish_row(i, coef):
        index = lax.broadcasted_iota(jnp.int32, (COEF, chans), 0)
        mode = jnp.where(index < CMAX, index, index - CMAX)
        coef = jnp.where(mode < cuts[i], coef, 0.0)
        high = coef.astype(jnp.bfloat16).astype(jnp.float32)
        low = coef - high
        zeros = jnp.zeros((256 - 3 * COEF, chans), jnp.float32)
        right = jnp.concatenate([high, high, low, zeros], axis=0).astype(jnp.bfloat16)
        smoothed = jnp.dot(inv[...], right, preferred_element_type=jnp.float32)
        stage[i] = stage[i] - smoothed[:cols]
        send_row(i)

    @pl.when(jnp.logical_not(polar))
    def _():
        def body(i, carry):
            plain_row(i)
            return carry

        lax.fori_loop(1, rows - 1, body, 0)
        wait_ghost(0)
        wait_ghost(1)
        plain_row(0)
        plain_row(rows - 1)

    @pl.when(polar)
    def _():
        def polar_row(n):
            return (1 - last) * (POLAR - 1 - n) + last * (rows - POLAR + n)

        plain = rows - POLAR

        def other_row(n):
            return (1 - last) * (POLAR + n) + last * (plain - 1 - n)

        def part_copy(k):
            return remote(part.at[k], part_in.at[k], part_send.at[k], part_recv.at[k], lat, sibling)

        def outward_in(k):
            return remote(acc.at[k], from_outer.at[k], inner_send.at[k], outer_recv.at[k], lat, inner)

        def across(k):
            return remote(acc.at[k], from_inner.at[k], inner_send.at[k], inner_recv.at[k], lat, inner)

        def outward(k):
            return remote(total.at[k], from_inner.at[k], outer_send.at[k], inner_recv.at[k], lat, outer)

        def total_copy(k):
            return remote(total.at[k], other_total.at[k], tot_send.at[k], tot_recv.at[k], lat, sibling)

        pltpu.make_async_copy(fwd_hbm.at[lon], fwd, tab_sem.at[0]).wait()
        pltpu.make_async_copy(inv_hbm.at[lon], inv, tab_sem.at[1]).wait()

        def send_inner(k):
            @pl.when(innermost)
            def _():
                across(k).start()

            @pl.when(jnp.logical_not(innermost))
            def _():
                outward_in(k).start()

        def join_pair(k):
            part_copy(k).wait_recv()
            acc[k] = acc[k] + part_in[k]

            @pl.when(depth == 0)
            def _():
                send_inner(k)

        def forward(k, carry):
            @pl.when(k == CHUNKS - 1)
            def _():
                @pl.when(lat == 0)
                def _():
                    wait_ghost(0)
                    flip_ghost(0)

                @pl.when(lat == lat_count - 1)
                def _():
                    wait_ghost(1)
                    flip_ghost(rows + 1)

            part[k] = coefficients(polar_row(2 * k + 1 - core))
            part_copy(k).start()
            acc[k] = coefficients(polar_row(2 * k + core))

            @pl.when(k > 0)
            def _():
                join_pair(k - 1)

            return carry

        lax.fori_loop(0, CHUNKS, forward, 0)
        join_pair(CHUNKS - 1)

        def middle(k, carry):
            @pl.when(depth > 0)
            def _():
                outward_in(k).wait_recv()
                acc[k] = acc[k] + from_outer[k]
                send_inner(k)

            @pl.when(k == CHUNKS - 1)
            def _():
                @pl.when(lat == 0)
                def _():
                    wait_ghost(1)

                @pl.when(lat == lat_count - 1)
                def _():
                    wait_ghost(0)

            def one(n, inside):
                plain_row(other_row(n))
                return inside

            return lax.fori_loop(k * plain // CHUNKS, (k + 1) * plain // CHUNKS, one, carry)

        lax.fori_loop(0, CHUNKS, middle, 0)

        def finish(k):
            total_copy(k).wait_recv()
            finish_row(polar_row(2 * k + core), total[k])
            finish_row(polar_row(2 * k + 1 - core), other_total[k])

        def backward(k, carry):
            across(k).wait_recv()
            received = from_inner[k]
            total[k] = jnp.where(innermost, received + acc[k], received)
            total_copy(k).start()

            @pl.when(depth > 0)
            def _():
                outward(k).start()

            @pl.when(k > 0)
            def _():
                finish(k - 1)

            return carry

        lax.fori_loop(0, CHUNKS, backward, 0)
        finish(CHUNKS - 1)

        def drain(k, carry):
            part_copy(k).wait_send()
            across(k).wait_send()
            total_copy(k).wait_send()

            @pl.when(depth > 0)
            def _():
                outward(k).wait_send()

            return carry

        lax.fori_loop(0, CHUNKS, drain, 0)

    to_west.wait_send()
    to_east.wait_send()
    for slot in range(2):
        row_copy(0, 0, slot, slot, lat, behind).wait_send()
    pltpu.make_async_copy(stage, out, out_sem).wait()


def local(forward, inverse, table, lat_count, lon_count, atmosphere, cutoff_table):
    rows, cols, chans = atmosphere.shape
    coef = pltpu.VMEM((CHUNKS, COEF, chans), jnp.float32)
    any_space = pl.BlockSpec(memory_space=pl.ANY)
    scalars = pl.BlockSpec(memory_space=pltpu.SMEM)
    dma = pltpu.SemaphoreType.DMA
    return pl.pallas_call(
        functools.partial(kernel, lat_count, lon_count, chans // 8),
        out_shape=jax.ShapeDtypeStruct(atmosphere.shape, atmosphere.dtype),
        in_specs=[any_space, scalars, scalars, any_space, any_space],
        out_specs=any_space,
        scratch_shapes=[
            pltpu.VMEM((rows + 2, cols + 2 * PAD, chans), jnp.float32),
            pltpu.VMEM((rows, cols, chans), jnp.float32),
            pltpu.VMEM((cols, chans), jnp.float32),
            pltpu.VMEM(forward.shape[1:], jnp.bfloat16),
            pltpu.VMEM(inverse.shape[1:], jnp.bfloat16),
            pltpu.VMEM((2, rows, 1, chans), jnp.float32),
            pltpu.VMEM((2, rows, 1, chans), jnp.float32),
            coef, coef, coef, coef, coef, coef, coef,
            dma, dma, dma((2,)), dma((2,)), dma((2,)), dma((2,)), dma((2,)),
        ] + [dma((CHUNKS,))] * 8,
        compiler_params=pltpu.CompilerParams(
            collective_id=0, has_side_effects=True, vmem_limit_bytes=48 * 1024 * 1024
        ),
    )(atmosphere, cutoff_table, table, forward, inverse)


def solution(mesh):
    lat_count, lon_count = mesh.shape["lat"], mesh.shape["lon"]

    def whole(atmosphere, cutoff_table):
        total_lat, total_lon, _ = atmosphere.shape
        forward, inverse = fourier_tables(lon_count, total_lon // lon_count)
        body = functools.partial(
            local, jnp.asarray(forward), jnp.asarray(inverse),
            jnp.asarray(row_table(total_lat)), lat_count, lon_count,
        )
        return jax.shard_map(
            body, mesh=mesh, in_specs=(P("lat", "lon", None), P("lat")),
            out_specs=P("lat", "lon", None), check_vma=False,
        )(atmosphere, cutoff_table)

    return whole
```

time: 637 us -> 64.6 us (0.10)
  waiting for transfers between devices: 334 us -> 0 us
  local copies, waits for them, and re-layouts: 148 us -> 9.68 us
  other arithmetic: 99.3 us -> 0 us
  Pallas kernels: 0 us -> 54.1 us
  matrix products: 31.5 us -> 0 us
  starting transfers between devices: 19.2 us -> 0 us
    all_to_all x2 -> x0, waiting for transfers between devices: 323 us -> none  [the longest x1 184 us: local(): lax.all_to_all(spread, 'lon', split_axis=2, concat_axis=1, tiled=True)]
    pallas_call x0 -> x1, Pallas kernels: none -> 54.1 us  [local(): pl.pallas_call(functools.partial(kernel, lat_count, lon_count, chans // 8...]
    all_to_all x4 -> x0, local copies, waits for them, and re-layouts: 40.1 us -> none  [the longest x2 21 us: local(): lax.all_to_all(spread, 'lon', split_axis=2, concat_axis=1, tiled=True)]
    unnamed x11 -> x9, local copies, waits for them, and re-layouts: 44.2 us -> 9.68 us
    unnamed x4 -> x0, matrix products: 31.5 us -> none
    mul x5 -> x0, other arithmetic: 23.8 us -> none  [the longest x1 17.2 us: local(): return atmosphere + time_step * (rest - filtered)]
    div x2 -> x0, other arithmetic: 22.9 us -> none  [the longest x1 22.9 us: tendency_parts(): (courant_zonal * (flux_east - flux_west) + courant_meridional * (flux_nor...]
    select_n x1 -> x0, local copies, waits for them, and re-layouts: 20.4 us -> none  [filter_circles(): return jnp.where((cuts >= count // 2)[:, None, None], circles, smoothed)]
  transfers between devices with their start and end apart: 7 -> 0, of which waited for: 5 -> 0; matrix products, arithmetic and copies ran while one was open for 5% -> 0% of each run, Pallas kernels for 0% -> 0%
where the time goes in v1:
time: 64.6 us; the launch traced here: 63.8 us
  Pallas kernels  54.1 us (84%)
  local copies, waits for them, and re-layouts  9.68 us (15%)
    pallas_call x1, Pallas kernels, local(): pl.pallas_call(functools.partial(kernel, lat_count, lon_count, chans // 8...  54.1 us
    unnamed x9, local copies, waits for them, and re-layouts  9.68 us

profile of v1, /device:TPU:0, one launch (start us, length us, event | category | flops | bytes accessed | tf_op | source)
XLA Modules:
  0.0 63.8 jit_solution(10905486375724294524)
XLA Ops:
  0.0 0.0 copy-start
  0.0 1.1 %copy-done = bf16[8,192,256]{2,1,0:T(8,128)(2,1)S(1)} copy-done((bf16[8,192,256]{2,1,0:T(8,128)(2,1)S(1)}, bf16[8,192,256]{2,1,0:T(8,128)(2,1)}, u32[]{:S(2)}) %copy-start) | copy-done | bytes 786456
  1.1 0.0 copy-start.1
  1.1 1.1 %copy-done.1 = bf16[8,144,192]{2,1,0:T(8,128)(2,1)S(1)} copy-done((bf16[8,144,192]{2,1,0:T(8,128)(2,1)S(1)}, bf16[8,144,192]{2,1,0:T(8,128)(2,1)}, u32[]{:S(2)}) %copy-start.1) | copy-done | bytes 442392
  2.2 0.0 copy-start.2
  2.2 0.7 %copy-done.2 = f32[512]{0:T(512)S(1)} copy-done((f32[512]{0:T(512)S(1)}, f32[512]{0:T(512)}, u32[]{:S(2)}) %copy-start.2) | copy-done | bytes 2072
  2.9 0.0 copy-start.3
  2.9 0.7 %copy-done.3 = s32[32]{0:T(128)S(1)} copy-done((s32[32]{0:T(128)S(1)}, s32[32]{0:T(128)}, u32[]{:S(2)}) %copy-start.3) | copy-done | bytes 152
  3.5 54.1 %shard_map.55 = f32[32,192,256]{2,1,0:T(8,128)} custom-call(f32[32,192,256]{2,1,0:T(8,128)} %atm.1, s32[32]{0:T(128)S(1)} %copy-done.3, f32[512]{0:T(512)S(1)} %copy-done.2, bf16[8,144,192]{2,1,0:T(8,128)(2,1)S(1)} %copy-done.1, bf16[8,192,256]{2,1,0:T(8,128)(2,1)S(1)} %copy-done), custom_call_target="tpu_custom_call" | custom-call | tf_op jit(solution)/shard_map/pallas_call | solution.py:399
  57.6 6.1 %copy.7 = f32[32,192,256]{2,1,0:T(8,128)} copy(f32[32,192,256]{2,1,0:T(8,128)} %shard_map.55) | data formatting | bytes 12582912
Async XLA Ops:
  0.0 1.1 %copy-start = (bf16[8,192,256]{2,1,0:T(8,128)(2,1)S(1)}, bf16[8,192,256]{2,1,0:T(8,128)(2,1)}, u32[]{:S(2)}) copy-start(bf16[8,192,256]{2,1,0:T(8,128)(2,1)} %constant.8.clone.inv_hbm) | copy-start | bytes 2359300
  1.1 1.1 %copy-start.1 = (bf16[8,144,192]{2,1,0:T(8,128)(2,1)S(1)}, bf16[8,144,192]{2,1,0:T(8,128)(2,1)}, u32[]{:S(2)}) copy-start(bf16[8,144,192]{2,1,0:T(8,128)(2,1)} %constant.7.clone.fwd_hbm) | copy-start | bytes 1327108
  2.2 0.7 %copy-start.2 = (f32[512]{0:T(512)S(1)}, f32[512]{0:T(512)}, u32[]{:S(2)}) copy-start(f32[512]{0:T(512)} %constant.6.clone.table) | copy-start | bytes 6148
  2.9 0.7 %copy-start.3 = (s32[32]{0:T(128)S(1)}, s32[32]{0:T(128)}, u32[]{:S(2)}) copy-start(s32[32]{0:T(128)} %cuts.1) | copy-start | bytes 388

commit v2 on v1

--- a/solution.py
+++ b/solution.py
@@ -13,7 +13,10 @@
 CMAX = 34
 POLAR = 16
 CHUNKS = POLAR // 2
+LAG_OUTER, LAG_TOTAL, LAG_FINISH, LAG_PLAIN = 3, 7, 9, 8
 COEF = 72
+GROUP = 2
+BLOCK = 192
 PAD = 8
 MESH = pl.DeviceIdType.MESH
 
@@ -29,10 +32,10 @@
     spacing = np.pi / total_lat
     cos_mid = np.sin((rows + 0.5) * spacing)
     zonal = 0.25 * courant_zonal / cos_mid
-    north = 0.25 * courant_meridional * np.sin(rows * spacing) / cos_mid
-    south = 0.25 * courant_meridional * np.sin((rows + 1.0) * spacing) / cos_mid
+    north = 0.25 * courant_meridional * np.sin(rows * spacing)
+    south = 0.25 * courant_meridional * np.sin((rows + 1.0) * spacing)
     turning = time_step * coriolis_rate * np.cos((rows + 0.5) * spacing)
-    return np.concatenate([zonal, north, south, turning]).astype(np.float32)
+    return np.concatenate([zonal, north, turning, south]).astype(np.float32)
 
 
 def split16(values):
@@ -75,7 +78,7 @@
     rows, cols, chans = atm.shape
     lat, lon = lax.axis_index("lat"), lax.axis_index("lon")
     total_lat = lat_count * rows
-    block = math.gcd(cols, 48)
+    block = math.gcd(cols, BLOCK)
     chips = lon_count // 2
     half = chips // 2
     chip, core = lon // 2, lon % 2
@@ -156,14 +159,13 @@
     grid[1 : rows + 1, PAD - 1 : PAD, :] = ew_recv[0]
     grid[1 : rows + 1, PAD + cols : PAD + cols + 1, :] = ew_recv[1]
 
-    lane = lax.broadcasted_iota(jnp.int32, (block, 128), 1)
-    is_u = lane < levels
-    is_v = jnp.logical_and(lane >= levels, lane < 2 * levels)
-
-    def repeated(value, mask):
-        value = jnp.where(mask, value, 0.0)
-        value = value + pltpu.roll(value, levels, 1)
-        return value + pltpu.roll(value, 2 * levels, 1)
+    def tiled(zonal_wind, meridional_wind):
+        lane = lax.broadcasted_iota(jnp.int32, zonal_wind.shape, 1)
+        both = jnp.where(lane < levels, zonal_wind, meridional_wind)
+        both = jnp.where(lane < 2 * levels, both, pltpu.roll(both, 2 * levels, 1))
+        swapped = pltpu.roll(both, levels, 1)
+        even = (lane // levels) % 2 == 0
+        return jnp.where(even, both, swapped), jnp.where(even, swapped, both)
 
     def wait_ghost(side):
         row_copy(0, side * (rows + 1), side, side, lat, lon_count - 1 - lon).wait_recv()
@@ -173,52 +175,74 @@
         lanes = lax.broadcasted_iota(jnp.int32, (cols, 128), 1)
         grid[row, PAD : PAD + cols, 0:128] = jnp.where(lanes < 2 * levels, -winds, winds)
 
-    def row_step(i, filtered):
-        row = lat * rows + i
-        zonal = table[row]
-        north = table[total_lat + row]
-        south = table[2 * total_lat + row]
-        turn = table[3 * total_lat + row]
-        for first in range(PAD, PAD + cols, block):
-            winds = None
-            for h in range(chans // 128):
-                lanes = slice(h * 128, h * 128 + 128)
-                q = grid[i + 1, first : first + block, lanes]
-                q_n = grid[i, first : first + block, lanes]
-                q_s = grid[i + 2, first : first + block, lanes]
-                east = q + grid[i + 1, first + 1 : first + 1 + block, lanes]
-                west = q + grid[i + 1, first - 1 : first - 1 + block, lanes]
-                above = q + q_n
-                below = q + q_s
-                base = (1.0 - 4.0 * diffusion_rate * time_step) * q
-                base = base + (diffusion_rate * time_step) * (above + below)
-                if h == 0:
-                    winds = (
-                        repeated(zonal * east, is_u), repeated(zonal * west, is_u),
-                        repeated(north * above, is_v), repeated(south * below, is_v),
-                    )
-                    v = pltpu.roll(q, 128 - levels, 1)
-                    u = pltpu.roll(q, levels, 1)
-                    base = base + turn * jnp.where(is_u, v, jnp.where(is_v, -u, 0.0))
-                u_e, u_w, v_n, v_s = winds
-                value = (u_e * east - u_w * west) + (v_n * above - v_s * below)
-                columns = slice(first - PAD, first - PAD + block)
-                if filtered:
-                    stage[i, columns, lanes] = base
-                    spread[columns, lanes] = value
-                else:
-                    stage[i, columns, lanes] = base - time_step * value
+    halves = [slice(h * 128, h * 128 + 128) for h in range(chans // 128)]
+
+    def row_group(i, count, filtered):
+        scalars = []
+        for g in range(count):
+            row = lat * rows + i + g
+            scalars.append((table[row], table[total_lat + row], table[2 * total_lat + row]))
+        south = [table[3 * total_lat + lat * rows + i + g] for g in range(count)]
+        lane = lax.broadcasted_iota(jnp.int32, (1, 128), 1)
+        kept = [None] * count
+        for first in [0] + list(range(PAD, PAD + cols, block)):
+            width = block if first else PAD
+            own = slice(first, first + width)
+            shifted = slice(first + 1, first + 1 + width)
+            columns = slice(first - PAD, first - PAD + width)
+            above = face_above = None
+            if first:
+                q_n = [grid[i, own, h] for h in halves]
+                q = [grid[i + 1, own, h] for h in halves]
+                above = [x + y for x, y in zip(q_n, q)]
+                scale = scalars[0][1]
+                _, v = tiled(above[0] * scale, above[0] * scale)
+                face_above = [v * x for x in above]
+            else:
+                q = [grid[i + 1, own, h] for h in halves]
+            for g in range(count):
+                zonal, _, turn = scalars[g]
+                east = [x + grid[i + 1 + g, shifted, h] for x, h in zip(q, halves)]
+                q_s = [grid[i + 2 + g, own, h] for h in halves]
+                below = [x + y for x, y in zip(q, q_s)]
+                u, v = tiled(east[0] * zonal, below[0] * south[g])
+                face_east = [u * x for x in east]
+                if first:
+                    face_below = [v * x for x in below]
+                    for n, h in enumerate(halves):
+                        joined = jnp.concatenate([kept[g][n], face_east[n]], axis=0)
+                        face_west = pltpu.roll(joined, 1, 0)[PAD:]
+                        value = (face_east[n] - face_west) + (face_above[n] - face_below[n]) * (
+                            4.0 / courant_zonal * zonal
+                        )
+                        base = (1.0 - 4.0 * diffusion_rate * time_step) * q[n]
+                        base = base + (diffusion_rate * time_step) * (above[n] + below[n])
+                        if n == 0:
+                            to_u = jnp.where(lane < levels, turn, 0.0)
+                            to_v = jnp.where(
+                                jnp.logical_and(lane >= levels, lane < 2 * levels), turn, 0.0
+                            )
+                            base = base + to_u * pltpu.roll(q[0], 128 - levels, 1)
+                            base = base - to_v * pltpu.roll(q[0], levels, 1)
+                        if filtered:
+                            stage[i + g, columns, h] = base
+                            spread[g, columns, h] = value
+                        else:
+                            stage[i + g, columns, h] = base - time_step * value
+                    above, face_above = below, face_below
+                kept[g] = [x[width - PAD :] for x in face_east]
+                q = q_s
 
     def send_row(i):
         pltpu.make_async_copy(stage.at[i], out.at[i], out_sem).start()
 
-    def plain_row(i):
-        row_step(i, False)
-        send_row(i)
-
-    def coefficients(i):
-        row_step(i, True)
-        value = spread[...]
+    def plain_rows(i):
+        row_group(i, GROUP, False)
+        for g in range(GROUP):
+            send_row(i + g)
+
+    def coefficients(g):
+        value = spread[g]
         high = value.astype(jnp.bfloat16)
         low = (value - high.astype(jnp.float32)).astype(jnp.bfloat16)
         weights = fwd[...]
@@ -241,14 +265,18 @@
     @pl.when(jnp.logical_not(polar))
     def _():
         def body(i, carry):
-            plain_row(i)
+            plain_rows(i * GROUP)
             return carry
 
-        lax.fori_loop(1, rows - 1, body, 0)
+        lax.fori_loop(1, rows // GROUP - 1, body, 0)
         wait_ghost(0)
         wait_ghost(1)
-        plain_row(0)
-        plain_row(rows - 1)
+
+        def end(n, carry):
+            plain_rows(n * (rows - GROUP))
+            return carry
+
+        lax.fori_loop(0, 2, end, 0)
 
     @pl.when(polar)
     def _():
@@ -257,8 +285,10 @@
 
         plain = rows - POLAR
 
-        def other_row(n):
-            return (1 - last) * (POLAR + n) + last * (plain - 1 - n)
+        groups = plain // GROUP
+
+        def other_rows(n):
+            return (1 - last) * (POLAR + n * GROUP) + last * (plain - GROUP - n * GROUP)
 
         def part_copy(k):
             return remote(part.at[k], part_in.at[k], part_send.at[k], part_recv.at[k], lat, sibling)
@@ -295,7 +325,7 @@
             def _():
                 send_inner(k)
 
-        def forward(k, carry):
+        def forward(k):
             @pl.when(k == CHUNKS - 1)
             def _():
                 @pl.when(lat == 0)
@@ -308,67 +338,65 @@
                     wait_ghost(1)
                     flip_ghost(rows + 1)
 
-            part[k] = coefficients(polar_row(2 * k + 1 - core))
+            row_group((1 - last) * (POLAR - 2 - 2 * k) + last * (rows - POLAR + 2 * k), 2, True)
+            mine = (1 - last) * (1 - core) + last * core
+            part[k] = coefficients(1 - mine)
             part_copy(k).start()
-            acc[k] = coefficients(polar_row(2 * k + core))
-
-            @pl.when(k > 0)
-            def _():
-                join_pair(k - 1)
-
-            return carry
-
-        lax.fori_loop(0, CHUNKS, forward, 0)
-        join_pair(CHUNKS - 1)
-
-        def middle(k, carry):
+            acc[k] = coefficients(mine)
+
+        def join_outer(k):
             @pl.when(depth > 0)
             def _():
                 outward_in(k).wait_recv()
                 acc[k] = acc[k] + from_outer[k]
                 send_inner(k)
 
-            @pl.when(k == CHUNKS - 1)
-            def _():
-                @pl.when(lat == 0)
-                def _():
-                    wait_ghost(1)
-
-                @pl.when(lat == lat_count - 1)
-                def _():
-                    wait_ghost(0)
-
-            def one(n, inside):
-                plain_row(other_row(n))
-                return inside
-
-            return lax.fori_loop(k * plain // CHUNKS, (k + 1) * plain // CHUNKS, one, carry)
-
-        lax.fori_loop(0, CHUNKS, middle, 0)
+        def backward(k):
+            across(k).wait_recv()
+            received = from_inner[k]
+            total[k] = jnp.where(innermost, received + acc[k], received)
+            total_copy(k).start()
+
+            @pl.when(depth > 0)
+            def _():
+                outward(k).start()
 
         def finish(k):
             total_copy(k).wait_recv()
             finish_row(polar_row(2 * k + core), total[k])
             finish_row(polar_row(2 * k + 1 - core), other_total[k])
 
-        def backward(k, carry):
-            across(k).wait_recv()
-            received = from_inner[k]
-            total[k] = jnp.where(innermost, received + acc[k], received)
-            total_copy(k).start()
-
-            @pl.when(depth > 0)
-            def _():
-                outward(k).start()
-
-            @pl.when(k > 0)
-            def _():
-                finish(k - 1)
+        def plain_part(k):
+            @pl.when(k == CHUNKS - 1)
+            def _():
+                @pl.when(lat == 0)
+                def _():
+                    wait_ghost(1)
+
+                @pl.when(lat == lat_count - 1)
+                def _():
+                    wait_ghost(0)
+
+            def one(n, carry):
+                plain_rows(other_rows(n))
+                return carry
+
+            lax.fori_loop(k * groups // CHUNKS, (k + 1) * groups // CHUNKS, one, 0)
+
+        stages = (
+            (0, forward), (1, join_pair), (LAG_OUTER, join_outer), (LAG_PLAIN, plain_part),
+            (LAG_TOTAL, backward), (LAG_FINISH, finish),
+        )
+
+        def tick(t, carry):
+            for lag, stage_of in stages:
+                @pl.when(jnp.logical_and(t >= lag, t < lag + CHUNKS))
+                def _():
+                    stage_of(t - lag)
 
             return carry
 
-        lax.fori_loop(0, CHUNKS, backward, 0)
-        finish(CHUNKS - 1)
+        lax.fori_loop(0, CHUNKS + LAG_FINISH, tick, 0)
 
         def drain(k, carry):
             part_copy(k).wait_send()
@@ -404,7 +432,7 @@
         scratch_shapes=[
             pltpu.VMEM((rows + 2, cols + 2 * PAD, chans), jnp.float32),
             pltpu.VMEM((rows, cols, chans), jnp.float32),
-            pltpu.VMEM((cols, chans), jnp.float32),
+            pltpu.VMEM((2, cols, chans), jnp.float32),
             pltpu.VMEM(forward.shape[1:], jnp.bfloat16),
             pltpu.VMEM(inverse.shape[1:], jnp.bfloat16),
             pltpu.VMEM((2, rows, 1, chans), jnp.float32),
@@ -413,7 +441,7 @@
             dma, dma, dma((2,)), dma((2,)), dma((2,)), dma((2,)), dma((2,)),
         ] + [dma((CHUNKS,))] * 8,
         compiler_params=pltpu.CompilerParams(
-            collective_id=0, has_side_effects=True, vmem_limit_bytes=48 * 1024 * 1024
+            collective_id=0, has_side_effects=True, vmem_limit_bytes=60 * 1024 * 1024
         ),
     )(atmosphere, cutoff_table, table, forward, inverse)
 

time: 64.6 us -> 48.3 us (0.75); the launches traced: 63.8 us -> 48.1 us
  Pallas kernels: 54.1 us -> 42 us
  local copies, waits for them, and re-layouts: 9.68 us -> 6.15 us
    pallas_call x1, Pallas kernels: 54.1 us -> 42 us  [local(): pl.pallas_call(functools.partial(kernel, lat_count, lon_count, chans // 8...]
    unnamed x9 -> x1, local copies, waits for them, and re-layouts: 9.68 us -> 6.15 us
where the time goes in v2:
time: 48.3 us; the launch traced here: 48.1 us
  Pallas kernels  42 us (87%)
  local copies, waits for them, and re-layouts  6.15 us (13%)
    pallas_call x1, Pallas kernels, local(): pl.pallas_call(functools.partial(kernel, lat_count, lon_count, chans // 8...  42 us
    unnamed x1, local copies, waits for them, and re-layouts  6.15 us

profile of v2, /device:TPU:0, one launch (start us, length us, event | category | flops | bytes accessed | tf_op | source)
XLA Modules:
  0.0 48.1 jit_solution(1849121813684143967)
XLA Ops:
  0.0 42.0 %shard_map.55 = f32[32,192,256]{2,1,0:T(8,128)} custom-call(f32[32,192,256]{2,1,0:T(8,128)} %atm.1, s32[32]{0:T(128)} %cuts.1, f32[512]{0:T(512)} %constant.6.clone.table, bf16[8,144,192]{2,1,0:T(8,128)(2,1)} %constant.7.clone.fwd_hbm, bf16[8,192,256]{2,1,0:T(8,128)(2,1)} %constant.8.clone.inv_hbm), custom_call_target="tpu_custom_call" | custom-call | tf_op jit(solution)/shard_map/pallas_call | solution.py:427
  42.0 6.1 %copy.7 = f32[32,192,256]{2,1,0:T(8,128)} copy(f32[32,192,256]{2,1,0:T(8,128)} %shard_map.55) | data formatting | bytes 12582912

commit v3 on v2

--- a/solution.py
+++ b/solution.py
@@ -13,10 +13,11 @@
 CMAX = 34
 POLAR = 16
 CHUNKS = POLAR // 2
-LAG_OUTER, LAG_TOTAL, LAG_FINISH, LAG_PLAIN = 3, 7, 9, 8
+LAG_OUTER, LAG_TOTAL, LAG_FINISH, LAG_PLAIN = 4, 8, 11, 8
 COEF = 72
 GROUP = 2
 BLOCK = 192
+PIECES = 16
 PAD = 8
 MESH = pl.DeviceIdType.MESH
 
@@ -418,13 +419,30 @@
     pltpu.make_async_copy(stage, out, out_sem).wait()
 
 
+def write_out(source, out, held, in_sems, out_sems):
+    pieces = in_sems.shape[0]
+    size = source.shape[0] // pieces
+    loads, stores = [], []
+    for n in range(pieces):
+        part = pl.ds(n * size, size)
+        loads.append(pltpu.make_async_copy(source.at[part], held.at[part], in_sems.at[n]))
+        stores.append(pltpu.make_async_copy(held.at[part], out.at[part], out_sems.at[n]))
+    for load in loads:
+        load.start()
+    for load, store in zip(loads, stores):
+        load.wait()
+        store.start()
+    for store in stores:
+        store.wait()
+
+
 def local(forward, inverse, table, lat_count, lon_count, atmosphere, cutoff_table):
     rows, cols, chans = atmosphere.shape
     coef = pltpu.VMEM((CHUNKS, COEF, chans), jnp.float32)
     any_space = pl.BlockSpec(memory_space=pl.ANY)
     scalars = pl.BlockSpec(memory_space=pltpu.SMEM)
     dma = pltpu.SemaphoreType.DMA
-    return pl.pallas_call(
+    advanced = pl.pallas_call(
         functools.partial(kernel, lat_count, lon_count, chans // 8),
         out_shape=jax.ShapeDtypeStruct(atmosphere.shape, atmosphere.dtype),
         in_specs=[any_space, scalars, scalars, any_space, any_space],
@@ -444,6 +462,17 @@
             collective_id=0, has_side_effects=True, vmem_limit_bytes=60 * 1024 * 1024
         ),
     )(atmosphere, cutoff_table, table, forward, inverse)
+    pieces = math.gcd(rows, PIECES)
+    return pl.pallas_call(
+        write_out,
+        out_shape=jax.ShapeDtypeStruct(atmosphere.shape, atmosphere.dtype),
+        in_specs=[any_space],
+        out_specs=any_space,
+        scratch_shapes=[
+            pltpu.VMEM((rows, cols, chans), jnp.float32), dma((pieces,)), dma((pieces,)),
+        ],
+        compiler_params=pltpu.CompilerParams(vmem_limit_bytes=60 * 1024 * 1024),
+    )(advanced)
 
 
 def solution(mesh):

time: 48.3 us -> 46.9 us (0.971)
  local copies, waits for them, and re-layouts: 6.15 us -> 0 us
  Pallas kernels: 42 us -> 46.7 us
    unnamed x1 -> x0, local copies, waits for them, and re-layouts: 6.15 us -> none
    pallas_call x0 -> x1, Pallas kernels: none -> 5.48 us  [local(): pl.pallas_call(write_out, out_shape=jax.ShapeDtypeStruct(atmosphere.shape...]
    pallas_call x1, Pallas kernels: 42 us -> 41.2 us  [local(): pl.pallas_call(functools.partial(kernel, lat_count, lon_count, chans // 8...]
where the time goes in v3:
time: 46.9 us; the launch traced here: 46.7 us
  Pallas kernels  46.7 us (100%)
    pallas_call x1, Pallas kernels, local(): pl.pallas_call(functools.partial(kernel, lat_count, lon_count, chans // 8...  41.2 us
    pallas_call x1, Pallas kernels, local(): pl.pallas_call(write_out, out_shape=jax.ShapeDtypeStruct(atmosphere.shape...  5.48 us

profile of v3, /device:TPU:0, one launch (start us, length us, event | category | flops | bytes accessed | tf_op | source)
XLA Modules:
  0.0 46.7 jit_solution(7587072692674643159)
XLA Ops:
  0.0 41.2 %shard_map.55.source = f32[32,192,256]{2,1,0:T(8,128)} custom-call(f32[32,192,256]{2,1,0:T(8,128)} %atm.1, s32[32]{0:T(128)} %cuts.1, f32[512]{0:T(512)} %constant.6.clone.table, bf16[8,144,192]{2,1,0:T(8,128)(2,1)} %constant.7.clone.fwd_hbm, bf16[8,192,256]{2,1,0:T(8,128)(2,1)} %constant.8.clone.inv_hbm), custom_call_target="tpu_custom_call" | custom-call | tf_op jit(solution)/shard_map/pallas_call | solution.py:445
  41.2 5.5 %shard_map.56 = f32[32,192,256]{2,1,0:T(8,128)} custom-call(f32[32,192,256]{2,1,0:T(8,128)} %shard_map.55.source), custom_call_target="tpu_custom_call" | custom-call | tf_op jit(solution)/shard_map/pallas_call | solution.py:466

commit v4 on v3

--- a/solution.py
+++ b/solution.py
@@ -13,7 +13,7 @@
 CMAX = 34
 POLAR = 16
 CHUNKS = POLAR // 2
-LAG_OUTER, LAG_TOTAL, LAG_FINISH, LAG_PLAIN = 4, 8, 11, 8
+LAG_OUTER, LAG_TOTAL, LAG_FINISH, LAG_PLAIN = 5, 9, 12, 8
 COEF = 72
 GROUP = 2
 BLOCK = 192

time: 46.9 us -> 47.4 us (1.011)
  Pallas kernels: 46.7 us -> 47.2 us
    pallas_call x1, Pallas kernels: 41.2 us -> 41.8 us  [local(): pl.pallas_call(functools.partial(kernel, lat_count, lon_count, chans // 8...]
where the time goes in v4:
time: 47.4 us; the launch traced here: 47.3 us
  Pallas kernels  47.2 us (100%)
    pallas_call x1, Pallas kernels, local(): pl.pallas_call(functools.partial(kernel, lat_count, lon_count, chans // 8...  41.8 us
    pallas_call x1, Pallas kernels, local(): pl.pallas_call(write_out, out_shape=jax.ShapeDtypeStruct(atmosphere.shape...  5.48 us

profile of v4, /device:TPU:0, one launch (start us, length us, event | category | flops | bytes accessed | tf_op | source)
XLA Modules:
  0.0 47.3 jit_solution(1595586153199119838)
XLA Ops:
  0.0 41.8 %shard_map.55.source = f32[32,192,256]{2,1,0:T(8,128)} custom-call(f32[32,192,256]{2,1,0:T(8,128)} %atm.1, s32[32]{0:T(128)} %cuts.1, f32[512]{0:T(512)} %constant.6.clone.table, bf16[8,144,192]{2,1,0:T(8,128)(2,1)} %constant.7.clone.fwd_hbm, bf16[8,192,256]{2,1,0:T(8,128)(2,1)} %constant.8.clone.inv_hbm), custom_call_target="tpu_custom_call" | custom-call | tf_op jit(solution)/shard_map/pallas_call | solution.py:445
  41.8 5.5 %shard_map.56 = f32[32,192,256]{2,1,0:T(8,128)} custom-call(f32[32,192,256]{2,1,0:T(8,128)} %shard_map.55.source), custom_call_target="tpu_custom_call" | custom-call | tf_op jit(solution)/shard_map/pallas_call | solution.py:466
